TPU v7x, 32 devices: a whole 2x2x4 slice. The times are simulated.
32 devices in a mesh: group: 2 (over y), dp: 4 (over z), tensor: 4 (over x, core).
Axes of the slice: x: 2, y: 2, z: 4, core: 2. Of those that a mesh axis runs over, the one named last changes fastest.
Arguments:
- base_heads: bfloat16 [4096, 4096], P(('group', 'dp'), 'tensor'), parts along dimension 0, may hold values from -6 to 6
- source_heads: bfloat16 [4096, 4096], P(('group', 'dp'), 'tensor'), parts along dimension 0, may hold values from -6 to 6
- residual: bfloat16 [4096, 4096], P(('group', 'dp'), 'tensor'), parts along dimension 0, may hold values from -6 to 6
- weight: bfloat16 [4096, 4096], P('tensor', 'dp'), may hold values from -0.09375 to 0.09375
- cotangent: bfloat16 [4096, 4096], P(('group', 'dp')), parts along dimension 0, may hold values from -6 to 6
- send_slots: int32 [8, 4, 128], P(('group', 'dp')), parts along dimension 0, may hold values from -1 to 511, as said below
- recv_slots: int32 [8, 4, 128], P(('group', 'dp')), parts along dimension 0, may hold values from -1 to 511, as said below
- head_mask: int32 [32, 32], P(('group', 'dp'), 'tensor'), parts along dimension 0, may hold values 0 or 1
Outputs:
- layer_out: bfloat16 [4096, 4096], P(('group', 'dp'), 'tensor'), parts along dimension 0
- grad_base: bfloat16 [4096, 4096], P(('group', 'dp'), 'tensor'), parts along dimension 0
- grad_source: bfloat16 [4096, 4096], P(('group', 'dp'), 'tensor'), parts along dimension 0
- grad_weight: float32 [8192, 4096], P(('group', 'tensor'), 'dp'), parts along dimension 0
There are 2 independent parts, one for each index of `group`. A program takes and returns all parts, laid end to end along the dimension named above; an argument that names none is the same for every part. Nothing has to cross between parts.
Inputs may be any that keep to these rules, and one draw needn't show every extreme that they name: send_slots[i, j, k] is a row of dp index i's source tokens sent in slot k to dp index j, or -1 for an empty slot; live slots come first; no source row appears twice; between 1 and 128 slots are live for each i and j, and in every draw one dp index receives 128 rows from every dp index. recv_slots[j, i, k] is the row of dp index j's base tokens that takes the row sent in slot k from dp index i; it is -1 exactly where send_slots[i, j, k] is -1; no base row appears twice.
All inputs are finite; a program needn't handle non-finite values. No bound on the sum of `head_mask` on one device may be relied on, other than what follows from the above.
Results may differ from a plain program's by a relative error of at most 0.009.
Values may be sent and summed in bfloat16 or wider, within the bound.
A program may use at most 128 MiB of HBM per device.

v0:
```python
import jax
import jax.numpy as jnp
from jax import lax
from jax.sharding import PartitionSpec as P


def on_device(
    base_heads, source_heads, residual, weight, cotangent, send_slots, recv_slots, head_mask
):
    rows, width = base_heads.shape
    peers = send_slots.shape[1]
    slots = send_slots.shape[2]
    prompts, heads_here = head_mask.shape
    head_size = width // heads_here
    prompt_len = rows // prompts
    send_index = send_slots.reshape(-1)
    send_live = send_index >= 0
    outgoing = jnp.where(
        send_live[:, None], source_heads[jnp.maximum(send_index, 0)], jnp.zeros((), jnp.bfloat16)
    )
    arrived = lax.all_to_all(
        outgoing.reshape(peers, slots, width), "dp", split_axis=0, concat_axis=0, tiled=True
    ).reshape(peers * slots, width)
    recv_index = recv_slots.reshape(-1)
    recv_live = recv_index >= 0
    target = jnp.where(recv_live, recv_index, rows)
    incoming = jnp.zeros((rows, width), jnp.bfloat16).at[target].set(arrived, mode="drop")
    paired = jnp.zeros((rows,), jnp.int32).at[target].set(1, mode="drop")
    mask_rows = jnp.repeat(jnp.repeat(head_mask, prompt_len, axis=0), head_size, axis=1)
    choose = (paired[:, None] == 1) & (mask_rows == 1)
    mixed = jnp.where(choose, incoming, base_heads)
    partial_sum = jnp.dot(
        mixed, lax.all_gather(weight, "dp", axis=1, tiled=True), preferred_element_type=jnp.float32
    )
    attn = lax.psum_scatter(
        partial_sum.astype(jnp.bfloat16), "tensor", scatter_dimension=1, tiled=True
    ).astype(jnp.float32)
    layer_out = (attn + residual.astype(jnp.float32)).astype(jnp.bfloat16)
    grad_wide = lax.dot_general(
        cotangent,
        lax.all_gather(weight, "dp", axis=1, tiled=True),
        (((1,), (1,)), ((), ())),
        preferred_element_type=jnp.float32,
    )
    grad_mixed = grad_wide.astype(jnp.bfloat16)
    zero = jnp.zeros((), jnp.bfloat16)
    grad_base = jnp.where(choose, zero, grad_mixed)
    back_rows = jnp.where(recv_live, recv_index, 0)
    returned = jnp.where(recv_live[:, None] & choose[back_rows], grad_mixed[back_rows], zero)
    homeward = lax.all_to_all(
        returned.reshape(peers, slots, width), "dp", split_axis=0, concat_axis=0, tiled=True
    ).reshape(peers * slots, width)
    source_target = jnp.where(send_live, send_index, rows)
    grad_source = (
        jnp.zeros((rows, width), jnp.bfloat16).at[source_target].add(homeward, mode="drop")
    )
    grad_term = lax.dot_general(
        mixed, cotangent, (((0,), (0,)), ((), ())), preferred_element_type=jnp.float32
    )
    grad_weight = lax.psum_scatter(
        grad_term.astype(jnp.bfloat16), "dp", scatter_dimension=1, tiled=True
    ).astype(jnp.float32)
    return (layer_out, grad_base, grad_source, grad_weight)


def solution(mesh):
    return jax.shard_map(
        on_device,
        mesh=mesh,
        in_specs=(
            P(("group", "dp"), "tensor"),
            P(("group", "dp"), "tensor"),
            P(("group", "dp"), "tensor"),
            P("tensor", "dp"),
            P(("group", "dp"), None),
            P(("group", "dp"), None, None),
            P(("group", "dp"), None, None),
            P(("group", "dp"), "tensor"),
        ),
        out_specs=(
            P(("group", "dp"), "tensor"),
            P(("group", "dp"), "tensor"),
            P(("group", "dp"), "tensor"),
            P(("group", "tensor"), "dp"),
        ),
        check_vma=False,
    )
```

profile of v0, /device:TPU:3, one launch (start us, length us, event | category | flops | bytes accessed | tf_op | source)
XLA Modules:
  0.0 397.5 jit_solution(11213536541661268575)
XLA Ops:
  7.2 0.0 all-gather.2.cloned.1.call-start
  7.2 0.7 all-gather.2.cloned.1.call-update
  7.9 0.7 compare_select_fusion.3
  8.6 2.1 gather_fusion
  10.7 1.1 broadcast_select_fusion
  11.9 4.6 %all-to-all-start = ((bf16[4,128,1024]{2,1,0:T(8,128)(2,1)}), bf16[4,128,1024]{2,1,0:T(8,128)(2,1)S(1)}, u32[]{:S(2)}, u32[]{:S(2)}) async-start(bf16[4,128,1024]{2,1,0:T(8,128)(2,1)} %broadcast_select_fusion), calls=%async_computation | async-start | bytes 2097152 | tf_op jit(solution)/shard_map/all_to_all | solution.py:21
  16.5 2.4 scatter_custom_fusion
  19.0 48.9 %all-to-all-done = bf16[4,128,1024]{2,1,0:T(8,128)(2,1)S(1)} async-done(((bf16[4,128,1024]{2,1,0:T(8,128)(2,1)}), bf16[4,128,1024]{2,1,0:T(8,128)(2,1)S(1)}, u32[]{:S(2)}, u32[]{:S(2)}) %all-to-all-start) | async-done | bytes 1048608 | tf_op jit(solution)/shard_map/all_to_all | solution.py:21
  67.8 3.5 scatter_custom_fusion.1
  71.4 106.8 %all-gather.2.cloned.1.call-done = bf16[1024,4096]{1,0:T(8,128)(2,1)} async-done(((bf16[1024,1024]{1,0:T(8,128)(2,1)}), bf16[1024,4096]{1,0:T(8,128)(2,1)}) %all-gather.2.cloned.1.call-update) | async-done | bytes 8388624 | tf_op jit(solution)/shard_map/all_gather | solution.py:33
  178.3 1.6 broadcast_in_dim.41
  179.9 10.4 %broadcast_select_fusion.1 = (bf16[512,1024]{1,0:T(8,128)(2,1)}, pred[512,1024]{1,0:T(32,128)(4,1)S(1)}, bf16[512,1024]{1,0:T(8,128)(2,1)S(1)}) fusion(pred[64,8,8,128]{3,2,1,0:T(8,128)(4,1)S(1)} %bitcast.29, pred[512]{0:T(512)(128)(4,1)S(1)} %broadcast_compare_fusion, bf16[512,4096]{1,0:T(8,128)(2,1)} %param.12, ...), kind=kOutput, calls=%fused_computation.15 | convolution fusion | flops 4296540160 | bytes 15729152 | tf_op jit(solution)/shard_map/dot_general | solution.py:39
  190.4 6.1 %convolution_convert_fusion.1 = bf16[512,4096]{1,0:T(8,128)(2,1)} fusion(bf16[1024,4096]{1,0:T(8,128)(2,1)S(1)} %bitcast.39, pred[512,1024]{1,0:T(32,128)(4,1)S(1)} %get-tuple-element.5, bf16[512,1024]{1,0:T(8,128)(2,1)S(1)} %copy-done.1, bf16[512,1024]{1,0:T(8,128)(2,1)S(1)} %copy-done.5), kind=kOutput, calls=%fused_computation.7 | convolution fusion | flops 4297588736 | bytes 15204352 | tf_op jit(solution)/shard_map/dot_general | solution.py:32
  196.5 0.0 reduce-scatter.3.cloned.1.call-update
  196.5 0.2 reduce-scatter.5.cloned.1.call-start
  196.8 11.1 %convolution_convert_fusion = bf16[1024,4096]{1,0:T(8,128)(2,1)} fusion(bf16[512,4096]{1,0:T(8,128)(2,1)} %param.12, pred[512,1024]{1,0:T(32,128)(4,1)S(1)} %get-tuple-element.5, bf16[512,1024]{1,0:T(8,128)(2,1)} %scatter_custom_fusion.1, bf16[512,1024]{1,0:T(8,128)(2,1)} %param.8), kind=kOutput, calls=%fused_computation.6 | convolution fusion | flops 4299685888 | bytes 15204352 | tf_op jit(solution)/shard_map/dot_general | solution.py:57
  207.9 3.1 gather_fusion.1
  211.0 2.0 gather_fusion.2
  213.1 1.5 and_select_fusion
  214.6 27.9 %all_to_all.10 = bf16[4,128,1024]{2,1,0:T(8,128)(2,1)S(1)} all-to-all(bf16[4,128,1024]{2,1,0:T(8,128)(2,1)S(1)} %and_select_fusion), channel_id=1, replica_groups=mesh['group'=2,'dp'=4,'tensor'=4] {'dp'}, dimensions={0} | all-to-all | bytes 2097152 | tf_op jit(solution)/shard_map/all_to_all | solution.py:50
  242.5 5.9 %scatter_custom_fusion.2 = bf16[512,1024]{1,0:T(8,128)(2,1)} fusion(s32[512]{0:T(512)S(1)} %bitcast.35, bf16[512,1024]{1,0:T(8,128)(2,1)S(1)} %bitcast.28, bf16[]{:T(256)} %constant.7.clone.1), kind=kCustom, calls=%fused_computation.13 | custom fusion | flops 524288 | bytes 1048578 | tf_op jit(solution)/shard_map/scatter-add | solution.py:55
  248.4 3.5 add_convert_fusion
  251.9 135.0 %reduce-scatter.5.cloned.1.call-done = bf16[1024,1024]{1,0:T(8,128)(2,1)} async-done(((bf16[1024,4096]{1,0:T(8,128)(2,1)}), bf16[1024,1024]{1,0:T(8,128)(2,1)}) %reduce-scatter.5.cloned.1.call-update) | async-done | bytes 2097168 | tf_op jit(solution)/shard_map/reduce_scatter | solution.py:60
  386.9 4.1 %convert_element_type.27 = f32[1024,1024]{1,0:T(8,128)} convert(bf16[1024,1024]{1,0:T(8,128)(2,1)} %reduce-scatter.5.cloned.1.call-done) | non-fusion elementwise | flops 1048576 | bytes 6291456 | tf_op jit(solution)/shard_map/convert_element_type | solution.py:62
  (29 shorter events, 0.1 us)
Async XLA Ops:
  7.2 1.5 copy-start
  7.2 171.0 %all-gather.2.cloned.1.call-start = ((), (), s32[]{:S(2)}) async-start(), calls=%async_computation.4 | async-start | bytes 10485760 | tf_op jit(solution)/shard_map/all_gather | solution.py:33
  8.6 2.1 copy-start.2
  10.7 5.7 %copy-start.3 = (s32[1,4,128]{2,1,0:T(4,128)S(1)}, s32[1,4,128]{2,1,0:T(4,128)}, u32[]{:S(2)}) copy-start(s32[1,4,128]{2,1,0:T(4,128)} %param.14) | copy-start | bytes 6148
  10.7 8.2 %copy-start.4 = (s32[4,8]{1,0:T(4,128)S(1)}, s32[4,8]{1,0:T(4,128)}, u32[]{:S(2)}) copy-start(s32[4,8]{1,0:T(4,128)} %param.15) | copy-start | bytes 388
  11.9 56.0 %all-to-all-start = ((bf16[4,128,1024]{2,1,0:T(8,128)(2,1)}), bf16[4,128,1024]{2,1,0:T(8,128)(2,1)S(1)}, u32[]{:S(2)}, u32[]{:S(2)}) async-start(bf16[4,128,1024]{2,1,0:T(8,128)(2,1)} %broadcast_select_fusion), calls=%async_computation | async-start | bytes 2097152 | tf_op jit(solution)/shard_map/all_to_all | solution.py:21
  16.5 232.0 %reduce-scatter.3.cloned.1.call-start = ((), (), s32[]{:S(2)}) async-start(), calls=%async_computation.5 | async-start | bytes 5242880 | tf_op jit(solution)/shard_map/reduce_scatter | solution.py:35
  178.2 12.1 %slice-start = ((s8[8388608]{0:T(1024)(128)(4,1)}), s8[4194304]{0:T(1024)(128)(4,1)S(1)}, s32[]{:S(2)}) async-start(s8[8388608]{0:T(1024)(128)(4,1)} %bitcast.38), calls=%async_computation.7 | async-start | bytes 8388608
  179.9 10.5 %copy-start.1 = (bf16[512,1024]{1,0:T(8,128)(2,1)S(1)}, bf16[512,1024]{1,0:T(8,128)(2,1)}, u32[]{:S(2)}) copy-start(bf16[512,1024]{1,0:T(8,128)(2,1)} %scatter_custom_fusion.1) | copy-start | bytes 3145732
  179.9 10.5 %slice-start.1 = ((s8[8388608]{0:T(1024)(128)(4,1)}), s8[4194304]{0:T(1024)(128)(4,1)S(1)}, s32[]{:S(2)}) async-start(s8[8388608]{0:T(1024)(128)(4,1)} %bitcast.38), calls=%async_computation.8 | async-start | bytes 8388608
  179.9 10.5 %copy-start.5 = (bf16[512,1024]{1,0:T(8,128)(2,1)S(1)}, bf16[512,1024]{1,0:T(8,128)(2,1)}, u32[]{:S(2)}) copy-start(bf16[512,1024]{1,0:T(8,128)(2,1)} %param.8) | copy-start | bytes 3145732
  196.5 190.4 %reduce-scatter.5.cloned.1.call-start = ((), (), s32[]{:S(2)}) async-start(), calls=%async_computation.6 | async-start | bytes 10485760 | tf_op jit(solution)/shard_map/reduce_scatter | solution.py:60
Sparse Core Ops, SparseCore 0:
  9.6 168.5 all-gather.1
  196.6 42.3 reduce-scatter.2
  241.6 145.2 reduce-scatter.4
where the time goes:
time: 399 us; the launch traced here: 398 us
  waiting for transfers between devices  291 us (73%)
  blocking collectives  27.9 us (7%)
  matrix products  27.7 us (7%)
  other arithmetic  16.8 us (4%)
  local copies, waits for them, and re-layouts  14.9 us (4%)
  between operations  13.9 us (3%)
  starting transfers between devices  4.85 us (1%)
    reduce_scatter x1, waiting for transfers between devices, on_device(): lax.psum_scatter(grad_term.astype(jnp.bfloat16), 'dp', scatter_dimension=...  135 us
    all_gather x1, waiting for transfers between devices, on_device(): lax.all_gather(weight, 'dp', axis=1, tiled=True)  107 us
    all_to_all x1, waiting for transfers between devices, on_device(): lax.all_to_all(outgoing.reshape(peers, slots, width), 'dp', split_axis=0,...  48.9 us
    all_to_all x1, blocking collectives, on_device(): lax.all_to_all(returned.reshape(peers, slots, width), 'dp', split_axis=0,...  27.9 us
    dot_general x1, matrix products, on_device(): lax.dot_general(mixed, cotangent, (((0,), (0,)), ((), ())), preferred_ele...  11.1 us
    dot_general x1, matrix products, on_device(): lax.dot_general(cotangent, lax.all_gather(weight, 'dp', axis=1, tiled=Tru...  10.4 us
  transfers between devices with their start and end apart: 4, of which 3 were waited for; matrix products, arithmetic and copies ran while one was open for 9% of the time, Pallas kernels for 0%

commit v1 on v0

--- a/solution.py
+++ b/solution.py
@@ -1,10 +1,14 @@
+import functools
+
 import jax
 import jax.numpy as jnp
 from jax import lax
+from jax.experimental import pallas as pl
+from jax.experimental.pallas import tpu as pltpu
 from jax.sharding import PartitionSpec as P
 
 
-def on_device(
+def with_collectives(
     base_heads, source_heads, residual, weight, cotangent, send_slots, recv_slots, head_mask
 ):
     rows, width = base_heads.shape
@@ -63,9 +67,430 @@
     return (layer_out, grad_base, grad_source, grad_weight)
 
 
+MESH = pl.DeviceIdType.MESH
+TILE = 256
+
+
+def nn(a, b):
+    return jnp.dot(a, b, preferred_element_type=jnp.float32)
+
+
+def nt(a, b):
+    return lax.dot_general(a, b, (((1,), (1,)), ((), ())), preferred_element_type=jnp.float32)
+
+
+def tn(a, b):
+    return lax.dot_general(a, b, (((0,), (0,)), ((), ())), preferred_element_type=jnp.float32)
+
+
+def fused(
+    n,
+    weight_ref,
+    cotangent_ref,
+    residual_ref,
+    base_ref,
+    source_ref,
+    choose_ref,
+    pick_ref,
+    place_ref,
+    pick_back_ref,
+    place_back_ref,
+    layer_ref,
+    grad_base_ref,
+    grad_source_ref,
+    grad_weight_ref,
+    w_all,
+    cot_own,
+    cot_all,
+    mixed_all,
+    rows_out,
+    rows_in,
+    home_ref,
+    part_out,
+    part_in,
+    grad_acc,
+    res_v,
+    local_sem,
+    w_send,
+    w_recv,
+    y_send,
+    y_recv,
+    m_send,
+    m_recv,
+    s_send,
+    s_recv,
+    h_send,
+    h_recv,
+    c_send,
+    c_recv,
+    b_send,
+    p_send,
+    p_recv,
+):
+    g = lax.axis_index("group")
+    i = lax.axis_index("dp")
+    t = lax.axis_index("tensor")
+    tokens, width = base_ref.shape
+    half = w_all.shape[1] // 2
+    block = w_all.shape[2]
+    slots = rows_out.shape[0] // n
+    quarter = tokens // n
+
+    def remote(src, dst, send, recv, to):
+        return pltpu.make_async_remote_copy(
+            src_ref=src, dst_ref=dst, send_sem=send, recv_sem=recv, device_id=to, device_id_type=MESH
+        )
+
+    def columns(k):
+        return pl.ds(pl.multiple_of(k * TILE, TILE), TILE)
+
+    def mine():
+        return pl.ds(pl.multiple_of(g * half, half), half)
+
+    def theirs():
+        return pl.ds(pl.multiple_of((1 - g) * half, half), half)
+
+    def strip(k):
+        return pl.ds(pl.multiple_of(k * quarter, quarter), quarter)
+
+    def slot_rows(k):
+        return pl.ds(pl.multiple_of(k * slots, slots), slots)
+
+    def w_first(side):
+        to = jnp.clip(i + 1 - 2 * side, 0, n - 1)
+        return remote(
+            weight_ref.at[mine(), :], w_all.at[i, mine(), :], w_send.at[side, i], w_recv.at[i], {"dp": to}
+        )
+
+    def w_pass(side, s):
+        to = jnp.clip(i + 1 - 2 * side, 0, n - 1)
+        return remote(
+            w_all.at[s, mine(), :], w_all.at[s, mine(), :], w_send.at[side, s], w_recv.at[s], {"dp": to}
+        )
+
+    def w_across(s):
+        return remote(
+            w_all.at[s, mine(), :], w_all.at[s, mine(), :], y_send.at[s], y_recv.at[s], {"group": 1 - g}
+        )
+
+    def w_across_in(s):
+        return remote(
+            w_all.at[s, theirs(), :], w_all.at[s, theirs(), :], y_send.at[s], y_recv.at[s], {"group": 1 - g}
+        )
+
+    def m_pass(side, s):
+        to = jnp.clip(i + 1 - 2 * side, 0, n - 1)
+        return remote(mixed_all.at[s], mixed_all.at[s], m_send.at[side, s], m_recv.at[s], {"dp": to})
+
+    def rows_to(j):
+        return remote(rows_out.at[slot_rows(j), :], rows_in.at[slot_rows(i), :], s_send.at[j], s_recv.at[i], {"dp": j})
+
+    def rows_from(j):
+        return remote(rows_out.at[slot_rows(j), :], rows_in.at[slot_rows(j), :], s_send.at[j], s_recv.at[j], {"dp": j})
+
+    def rows_home(j):
+        return remote(rows_out.at[slot_rows(j), :], home_ref.at[slot_rows(i), :], h_send.at[j], h_recv.at[i], {"dp": j})
+
+    def rows_home_in(j):
+        return remote(rows_out.at[slot_rows(j), :], home_ref.at[slot_rows(j), :], h_send.at[j], h_recv.at[j], {"dp": j})
+
+    def cot_to(j):
+        where = pl.ds(pl.multiple_of(j * block, block), block)
+        return remote(
+            cotangent_ref.at[strip(t), where], cot_all.at[i, strip(t), :], c_send.at[j], c_recv.at[i, t], {"dp": j}
+        )
+
+    def cot_share(j, u):
+        return remote(
+            cot_all.at[j, strip(t), :], cot_all.at[j, strip(t), :], b_send.at[j, u], c_recv.at[j, t], {"tensor": u}
+        )
+
+    def cot_in(j, u):
+        return remote(
+            cot_all.at[j, strip(u), :], cot_all.at[j, strip(u), :], b_send.at[j, u], c_recv.at[j, u], {"tensor": u}
+        )
+
+    def part_to(u):
+        return remote(part_out.at[u], part_in.at[t], p_send.at[u], p_recv.at[t], {"tensor": u})
+
+    def part_from(u):
+        return remote(part_out.at[u], part_in.at[u], p_send.at[u], p_recv.at[u], {"tensor": u})
+
+    def others(me, body):
+        def step(k, carry):
+            body(lax.rem(me + k, n))
+            return carry
+
+        lax.fori_loop(1, n, step, 0)
+
+    def at_distance(k, body):
+        for side in range(2):
+            s = i - k if side == 0 else i + k
+            inside = (s >= 0) & (s < n)
+            onward = inside & ((i + 1 < n) if side == 0 else (i >= 1))
+            body(side, jnp.clip(s, 0, n - 1), inside, onward)
+
+    loads = [pltpu.make_async_copy(weight_ref, w_all.at[i], local_sem.at[0])]
+    for k in range(n):
+        loads.append(
+            pltpu.make_async_copy(
+                cotangent_ref.at[:, k * block : (k + 1) * block], cot_own.at[k], local_sem.at[1 + k]
+            )
+        )
+    loads.append(pltpu.make_async_copy(residual_ref, res_v, local_sem.at[1 + n]))
+    for load in loads:
+        load.start()
+
+    barrier = pltpu.get_barrier_semaphore()
+    others(i, lambda j: pl.semaphore_signal(barrier, inc=1, device_id={"dp": j}, device_id_type=MESH))
+    others(t, lambda u: pl.semaphore_signal(barrier, inc=1, device_id={"tensor": u}, device_id_type=MESH))
+    pl.semaphore_signal(barrier, inc=1, device_id={"group": 1 - g}, device_id_type=MESH)
+
+    @pl.loop(0, width // TILE)
+    def _(k):
+        rows_out[:, columns(k)] = nn(pick_ref[...], source_ref[:, columns(k)]).astype(jnp.bfloat16)
+
+    pl.semaphore_wait(barrier, 2 * (n - 1) + 1)
+
+    others(i, lambda j: rows_to(j).start())
+
+    def start_w(side, s, inside, onward):
+        @pl.when(onward)
+        def _():
+            w_first(side).start()
+
+    at_distance(0, start_w)
+    others(i, lambda j: cot_to(j).start())
+    rows_in[slot_rows(i), :] = rows_out[slot_rows(i), :]
+
+    others(i, lambda j: rows_from(j).wait_recv())
+
+    @pl.loop(0, width // TILE)
+    def _(k):
+        c = columns(k)
+        incoming = nn(place_ref[...], rows_in[:, c])
+        chosen = choose_ref[:, c].astype(jnp.float32) > 0.5
+        mixed_all[i, :, c] = jnp.where(chosen, incoming, base_ref[:, c].astype(jnp.float32)).astype(jnp.bfloat16)
+        grad_acc[:, c] = jnp.zeros((tokens, TILE), jnp.float32)
+
+    def share_cot(j):
+        cot_to(j).wait_send()
+        cot_in(j, t).wait_recv()
+        others(t, lambda u: cot_share(j, u).start())
+
+    others(i, share_cot)
+    for load in loads:
+        load.wait()
+
+    def use_weight(s):
+        @pl.loop(0, width // TILE)
+        def _(k):
+            c = columns(k)
+            part_out[s, :, c] = nn(mixed_all[i], w_all[s, :, c]).astype(jnp.bfloat16)
+            grad_acc[:, c] += nt(cot_own[s], w_all[s, c, :])
+
+        @pl.when(s != t)
+        def _():
+            part_to(s).start()
+
+    def use_tokens(j):
+        @pl.loop(0, width // TILE)
+        def _(k):
+            c = columns(k)
+            grad_weight_ref[c, :] += tn(mixed_all[j, :, c], cot_all[j])
+
+    def round_of(k, carry):
+        def w_arrives(side, s, inside, onward):
+            @pl.when(inside & (k < n))
+            def _():
+                w_pass(side, s).wait_recv()
+                w_across(s).start()
+
+                @pl.when(onward)
+                def _():
+                    w_pass(side, s).start()
+
+        def m_arrives(side, s, inside, onward):
+            @pl.when(inside & (k >= 2))
+            def _():
+                m_pass(side, s).wait_recv()
+
+            @pl.when(onward)
+            def _():
+                m_pass(side, s).start()
+
+        def w_used(side, s, inside, onward):
+            first = inside if side == 0 else inside & (k >= 2)
+
+            @pl.when(first)
+            def _():
+                @pl.when(k >= 2)
+                def _():
+                    w_across_in(s).wait_recv()
+
+                use_weight(s)
+
+        at_distance(k, w_arrives)
+
+        @pl.when(k < n)
+        def _():
+            at_distance(k - 1, m_arrives)
+
+        at_distance(k - 1, w_used)
+        return carry
+
+    lax.fori_loop(1, n + 1, round_of, 0)
+
+    others(i, lambda j: rows_to(j).wait_send())
+
+    @pl.loop(0, width // TILE)
+    def _(k):
+        c = columns(k)
+        chosen = choose_ref[:, c].astype(jnp.float32) > 0.5
+        grad = grad_acc[:, c]
+        zero = jnp.zeros_like(grad)
+        grad_base_ref[:, c] = jnp.where(chosen, zero, grad).astype(jnp.bfloat16)
+        swapped = jnp.where(chosen, grad, zero).astype(jnp.bfloat16)
+        rows_out[:, c] = nn(pick_back_ref[...], swapped).astype(jnp.bfloat16)
+
+    others(i, lambda j: rows_home(j).start())
+    home_ref[slot_rows(i), :] = rows_out[slot_rows(i), :]
+
+    @pl.loop(0, width // TILE)
+    def _(k):
+        grad_weight_ref[columns(k), :] = tn(mixed_all[i, :, columns(k)], cot_own[i])
+
+    def tokens_of(k, carry):
+        def m_used(side, s, inside, onward):
+            @pl.when(inside)
+            def _():
+                @pl.when(k == n - 1)
+                def _():
+                    m_pass(side, s).wait_recv()
+
+                others(t, lambda u: cot_in(s, u).wait_recv())
+                use_tokens(s)
+
+        at_distance(k, m_used)
+        return carry
+
+    lax.fori_loop(1, n, tokens_of, 0)
+
+    others(t, lambda u: part_from(u).wait_recv())
+    part_in[t] = part_out[t]
+
+    @pl.loop(0, width // TILE)
+    def _(k):
+        c = columns(k)
+        total = res_v[:, c].astype(jnp.float32)
+        summed = part_in[0, :, c].astype(jnp.float32)
+        for u in range(1, n):
+            summed += part_in[u, :, c].astype(jnp.float32)
+        layer_ref[:, c] = (summed + total).astype(jnp.bfloat16)
+
+    others(i, lambda j: rows_home_in(j).wait_recv())
+
+    @pl.loop(0, width // TILE)
+    def _(k):
+        c = columns(k)
+        grad_source_ref[:, c] = nn(place_back_ref[...], home_ref[:, c]).astype(jnp.bfloat16)
+
+    others(i, lambda j: rows_home(j).wait_send())
+    others(t, lambda u: part_to(u).wait_send())
+    others(i, lambda j: others(t, lambda u: cot_share(j, u).wait_send()))
+
+    def drain(k, carry):
+        def sent(side, s, inside, onward):
+            @pl.when(onward)
+            def _():
+                w_pass(side, s).wait_send()
+                m_pass(side, s).wait_send()
+
+            @pl.when(inside & (k >= 1))
+            def _():
+                w_across(s).wait_send()
+
+        at_distance(k, sent)
+        return carry
+
+    lax.fori_loop(0, n, drain, 0)
+
+
+def with_kernel(
+    base_heads, source_heads, residual, weight, cotangent, send_slots, recv_slots, head_mask
+):
+    rows, width = base_heads.shape
+    n = send_slots.shape[1]
+    slots = n * send_slots.shape[2]
+    depth, block = weight.shape
+    prompts, heads_here = head_mask.shape
+    send_index = send_slots.reshape(-1)
+    recv_index = recv_slots.reshape(-1)
+    row = jnp.arange(rows, dtype=jnp.int32)
+    pick = (send_index[:, None] == row[None, :]).astype(jnp.bfloat16)
+    place_back = (row[:, None] == send_index[None, :]).astype(jnp.bfloat16)
+    place = (row[:, None] == recv_index[None, :]).astype(jnp.bfloat16)
+    pick_back = (recv_index[:, None] == row[None, :]).astype(jnp.bfloat16)
+    paired = jnp.any(row[:, None] == recv_index[None, :], axis=1)
+    swap = (paired.reshape(prompts, rows // prompts)[:, :, None] & (head_mask == 1)[:, None, :]).reshape(
+        rows, heads_here
+    )
+    choose = jnp.repeat(swap, width // heads_here, axis=1).astype(jnp.bfloat16)
+    kept = pl.BlockSpec(memory_space=pl.ANY)
+    near = pl.BlockSpec(memory_space=pltpu.VMEM)
+    dma = pltpu.SemaphoreType.DMA
+    bf16 = jnp.bfloat16
+    return pl.pallas_call(
+        functools.partial(fused, n),
+        out_shape=(
+            jax.ShapeDtypeStruct((rows, width), bf16),
+            jax.ShapeDtypeStruct((rows, width), bf16),
+            jax.ShapeDtypeStruct((rows, width), bf16),
+            jax.ShapeDtypeStruct((depth, block), jnp.float32),
+        ),
+        in_specs=[kept] * 3 + [near] * 7,
+        out_specs=(near,) * 4,
+        scratch_shapes=[
+            pltpu.VMEM((n, depth, block), bf16),
+            pltpu.VMEM((n, rows, block), bf16),
+            pltpu.VMEM((n, rows, block), bf16),
+            pltpu.VMEM((n, rows, width), bf16),
+            pltpu.VMEM((slots, width), bf16),
+            pltpu.VMEM((slots, width), bf16),
+            pltpu.VMEM((slots, width), bf16),
+            pltpu.VMEM((n, rows, block), bf16),
+            pltpu.VMEM((n, rows, block), bf16),
+            pltpu.VMEM((rows, width), jnp.float32),
+            pltpu.VMEM((rows, width), bf16),
+            dma((n + 2,)),
+            dma((2, n)),
+            dma((n,)),
+            dma((n,)),
+            dma((n,)),
+            dma((2, n)),
+            dma((n,)),
+            dma((n,)),
+            dma((n,)),
+            dma((n,)),
+            dma((n,)),
+            dma((n,)),
+            dma((n, n)),
+            dma((n, n)),
+            dma((n,)),
+            dma((n,)),
+        ],
+        compiler_params=pltpu.CompilerParams(
+            collective_id=0, has_side_effects=True, vmem_limit_bytes=60 * 1024 * 1024
+        ),
+    )(
+        weight, cotangent, residual, base_heads, source_heads, choose, pick, place, pick_back, place_back
+    )
+
+
 def solution(mesh):
+    square = mesh.shape["dp"] == mesh.shape["tensor"] and mesh.shape["group"] == 2
     return jax.shard_map(
-        on_device,
+        with_kernel if square else with_collectives,
         mesh=mesh,
         in_specs=(
             P(("group", "dp"), "tensor"),

time: 399 us -> 241 us (0.60)
  waiting for transfers between devices: 291 us -> 0 us
  Pallas kernels: 0 us -> 226 us
  blocking collectives: 27.9 us -> 0 us
  matrix products: 27.7 us -> 0 us
  other arithmetic: 16.8 us -> 3.28 us
  between operations: 13.9 us -> 0.66 us
  starting transfers between devices: 4.85 us -> 0 us
  local copies, waits for them, and re-layouts: 14.9 us -> 10.8 us
    pallas_call x0 -> x1, Pallas kernels: none -> 226 us  [with_kernel(): pl.pallas_call(functools.partial(fused, n), out_shape=(jax.ShapeDtypeStru...]
    reduce_scatter x2 -> x0, waiting for transfers between devices: 135 us -> none  [the longest x1 135 us: on_device(): lax.psum_scatter(grad_term.astype(jnp.bfloat16), 'dp', scatter_dimension=...]
    all_gather x1 -> x0, waiting for transfers between devices: 107 us -> none  [on_device(): lax.all_gather(weight, 'dp', axis=1, tiled=True)]
    all_to_all x1 -> x0, waiting for transfers between devices: 48.9 us -> none  [on_device(): lax.all_to_all(outgoing.reshape(peers, slots, width), 'dp', split_axis=0,...]
    all_to_all x1 -> x0, blocking collectives: 27.9 us -> none  [on_device(): lax.all_to_all(returned.reshape(peers, slots, width), 'dp', split_axis=0,...]
    dot_general x3 -> x0, matrix products: 27.7 us -> none  [the longest x1 11.1 us: on_device(): lax.dot_general(mixed, cotangent, (((0,), (0,)), ((), ())), preferred_ele...]
    unnamed x16 -> x7, local copies, waits for them, and re-layouts: 0.05 us -> 10.2 us
    gather x3 -> x0, local copies, waits for them, and re-layouts: 7.24 us -> none  [the longest x1 3.13 us: on_device(): choose[back_rows]]
  transfers between devices with their start and end apart: 4 -> 0, of which waited for: 3 -> 0; matrix products, arithmetic and copies ran while one was open for 9% -> 0% of each run, Pallas kernels for 0% -> 0%
where the time goes in v1:
time: 241 us; the launch traced here: 240 us
  Pallas kernels  226 us (94%)
  local copies, waits for them, and re-layouts  10.8 us (4%)
  other arithmetic  3.28 us (1%)
    pallas_call x1, Pallas kernels, with_kernel(): pl.pallas_call(functools.partial(fused, n), out_shape=(jax.ShapeDtypeStru...  226 us
    unnamed x7, local copies, waits for them, and re-layouts  10.2 us

profile of v1, /device:TPU:3, one launch (start us, length us, event | category | flops | bytes accessed | tf_op | source)
XLA Modules:
  0.0 240.5 jit_solution(1755613360648900091)
XLA Ops:
  0.6 0.7 broadcast_compare_fusion
  1.3 2.5 %fusion.3 = (bf16[512,512]{1,0:T(8,128)(2,1)}, bf16[512,512]{1,0:T(8,128)(2,1)}, pred[512]{0:T(512)(128)(4,1)S(1)}, bf16[512,512]{1,0:T(8,128)(2,1)}, bf16[512,512]{1,0:T(8,128)(2,1)}) fusion(s32[512]{0:T(512)} %bitcast.12, s32[512]{0:T(512)} %bitcast.13), kind=kLoop, calls=%fused_computation.8 | loop fusion | flops 2358784 | bytes 2101760 | tf_op jit(solution)/shard_map/convert_element_type | solution.py:433
  3.8 0.1 fusion.5
  3.9 0.6 broadcast_in_dim.2
  4.5 1.3 copy.14
  5.8 225.8 %shard_map.111 = (bf16[512,1024]{1,0:T(8,128)(2,1)}, bf16[512,1024]{1,0:T(8,128)(2,1)}, bf16[512,1024]{1,0:T(8,128)(2,1)}, f32[1024,1024]{1,0:T(8,128)}) custom-call(bf16[1024,1024]{1,0:T(8,128)(2,1)} %weight_ref.1, bf16[512,4096]{1,0:T(8,128)(2,1)} %cotangent_ref.1, bf16[512,1024]{1,0:T(8,128)(2,1)} %residual_ref.1, bf16[512,1024]{1,0:T(8,128)(2,1)} %base_ref.1, ...), custom_call_target="tpu_custom_call" | custom-call | tf_op jit(solution)/shard_map/pallas_call | solution.py:443
  231.5 0.0 copy-start
  231.5 2.4 %copy.19 = bf16[512,1024]{1,0:T(8,128)(2,1)} copy(bf16[512,1024]{1,0:T(8,128)(2,1)} %get-tuple-element.15) | data formatting | bytes 2097152
  234.0 2.3 copy.20
  236.2 2.3 copy.21
  238.5 0.0 copy-done
  238.5 2.0 copy.22
Async XLA Ops:
  231.5 7.0 %copy-start = (f32[1024,1024]{1,0:T(8,128)S(1)}, f32[1024,1024]{1,0:T(8,128)}, u32[]{:S(2)}) copy-start(f32[1024,1024]{1,0:T(8,128)} %get-tuple-element.18) | copy-start | bytes 12582916

commit v2 on v1

--- a/solution.py
+++ b/solution.py
@@ -90,11 +90,9 @@
     residual_ref,
     base_ref,
     source_ref,
-    choose_ref,
-    pick_ref,
-    place_ref,
-    pick_back_ref,
-    place_back_ref,
+    send_ref,
+    recv_ref,
+    heads_ref,
     layer_ref,
     grad_base_ref,
     grad_source_ref,
@@ -110,6 +108,12 @@
     part_in,
     grad_acc,
     res_v,
+    choose_v,
+    place_v,
+    back_v,
+    swapped_v,
+    end_out,
+    end_in,
     local_sem,
     w_send,
     w_recv,
@@ -126,6 +130,8 @@
     b_send,
     p_send,
     p_recv,
+    e_send,
+    e_recv,
 ):
     g = lax.axis_index("group")
     i = lax.axis_index("dp")
@@ -135,6 +141,9 @@
     block = w_all.shape[2]
     slots = rows_out.shape[0] // n
     quarter = tokens // n
+    middle = (i >= 1) & (i <= n - 2)
+    beside_end = (i == 1) | (i == n - 2)
+    end = jnp.where(i <= 1, 0, n - 1)
 
     def remote(src, dst, send, recv, to):
         return pltpu.make_async_remote_copy(
@@ -194,21 +203,35 @@
     def rows_home_in(j):
         return remote(rows_out.at[slot_rows(j), :], home_ref.at[slot_rows(j), :], h_send.at[j], h_recv.at[j], {"dp": j})
 
-    def cot_to(j):
-        where = pl.ds(pl.multiple_of(j * block, block), block)
+    def cot_to(b):
+        kind = 0 if 0 < b < n - 1 else 1
+        taker = min(max(b, 1), n - 2)
         return remote(
-            cotangent_ref.at[strip(t), where], cot_all.at[i, strip(t), :], c_send.at[j], c_recv.at[i, t], {"dp": j}
+            cotangent_ref.at[strip(t), b * block : (b + 1) * block],
+            cot_all.at[kind, i, strip(t), :],
+            c_send.at[b],
+            c_recv.at[kind, i, t],
+            {"dp": taker},
         )
 
-    def cot_share(j, u):
-        return remote(
-            cot_all.at[j, strip(t), :], cot_all.at[j, strip(t), :], b_send.at[j, u], c_recv.at[j, t], {"tensor": u}
-        )
-
-    def cot_in(j, u):
-        return remote(
-            cot_all.at[j, strip(u), :], cot_all.at[j, strip(u), :], b_send.at[j, u], c_recv.at[j, u], {"tensor": u}
-        )
+    def cot_sent(body):
+        for b in range(n):
+            taker = min(max(b, 1), n - 2)
+
+            @pl.when((i != b) & (i != taker))
+            def _():
+                body(cot_to(b))
+
+    def cot_share(kind, j, u):
+        piece = cot_all.at[kind, j, strip(t), :]
+        return remote(piece, piece, b_send.at[kind, j, u], c_recv.at[kind, j, t], {"tensor": u})
+
+    def cot_in(kind, j, u):
+        piece = cot_all.at[kind, j, strip(u), :]
+        return remote(piece, piece, b_send.at[kind, j, u], c_recv.at[kind, j, u], {"tensor": u})
+
+    def end_pass():
+        return remote(end_out, end_in, e_send.at[0], e_recv.at[0], {"dp": end})
 
     def part_to(u):
         return remote(part_out.at[u], part_in.at[t], p_send.at[u], p_recv.at[t], {"tensor": u})
@@ -246,9 +269,16 @@
     others(t, lambda u: pl.semaphore_signal(barrier, inc=1, device_id={"tensor": u}, device_id_type=MESH))
     pl.semaphore_signal(barrier, inc=1, device_id={"group": 1 - g}, device_id_type=MESH)
 
-    @pl.loop(0, width // TILE)
+    def hot(index):
+        count = place_v.shape[1]
+        equal = lax.broadcasted_iota(jnp.int32, (tokens, count), 0) == index
+        return jnp.where(equal, 1.0, 0.0)
+
+    back_v[...] = hot(send_ref[...]).astype(jnp.bfloat16)
+
+    @pl.loop(0, rows_out.shape[0] // TILE)
     def _(k):
-        rows_out[:, columns(k)] = nn(pick_ref[...], source_ref[:, columns(k)]).astype(jnp.bfloat16)
+        rows_out[columns(k), :] = tn(back_v[:, columns(k)], source_ref[...]).astype(jnp.bfloat16)
 
     pl.semaphore_wait(barrier, 2 * (n - 1) + 1)
 
@@ -260,27 +290,58 @@
             w_first(side).start()
 
     at_distance(0, start_w)
-    others(i, lambda j: cot_to(j).start())
+    cot_sent(lambda copy: copy.start())
     rows_in[slot_rows(i), :] = rows_out[slot_rows(i), :]
+    place = hot(recv_ref[...])
+    place_v[...] = place.astype(jnp.bfloat16)
+    paired = jnp.max(place, axis=1, keepdims=True)
+    prompts = heads_ref.shape[0]
+    length = tokens // prompts
+    for p in range(prompts):
+        rows = slice(p * length, (p + 1) * length)
+        choose_v[rows, :] = (paired[rows, :] * heads_ref[p : p + 1, :]).astype(jnp.bfloat16)
 
     others(i, lambda j: rows_from(j).wait_recv())
 
     @pl.loop(0, width // TILE)
     def _(k):
         c = columns(k)
-        incoming = nn(place_ref[...], rows_in[:, c])
-        chosen = choose_ref[:, c].astype(jnp.float32) > 0.5
+        incoming = nn(place_v[...], rows_in[:, c])
+        chosen = choose_v[:, c].astype(jnp.float32) > 0.5
         mixed_all[i, :, c] = jnp.where(chosen, incoming, base_ref[:, c].astype(jnp.float32)).astype(jnp.bfloat16)
         grad_acc[:, c] = jnp.zeros((tokens, TILE), jnp.float32)
 
-    def share_cot(j):
-        cot_to(j).wait_send()
-        cot_in(j, t).wait_recv()
-        others(t, lambda u: cot_share(j, u).start())
-
-    others(i, share_cot)
+    def m_onward(side, inside):
+        return inside & ((i + 1 <= n - 2) if side == 0 else (i - 1 >= 1))
+
+    def start_m(side, s, inside, onward):
+        @pl.when(m_onward(side, inside))
+        def _():
+            m_pass(side, s).start()
+
+    at_distance(0, start_m)
     for load in loads:
         load.wait()
+
+    def blocks_taken(body):
+        for kind in range(2):
+
+            @pl.when(middle if kind == 0 else beside_end)
+            def _():
+                def one(j):
+                    if kind == 0:
+                        body(kind, j)
+                    else:
+
+                        @pl.when(j != end)
+                        def _():
+                            body(kind, j)
+
+                others(i, one)
+
+    def share_cot(kind, j):
+        cot_in(kind, j, t).wait_recv()
+        others(t, lambda u: cot_share(kind, j, u).start())
 
     def use_weight(s):
         @pl.loop(0, width // TILE)
@@ -297,11 +358,36 @@
         @pl.loop(0, width // TILE)
         def _(k):
             c = columns(k)
-            grad_weight_ref[c, :] += tn(mixed_all[j, :, c], cot_all[j])
+            grad_weight_ref[c, :] += tn(mixed_all[j, :, c], cot_all[0, j])
+
+    def end_terms():
+        blocks_taken(lambda kind, j: others(t, lambda u: cot_in(kind, j, u).wait_recv()))
+        first = lax.rem(end + 1, n)
+        second = lax.rem(end + 2, n)
+        third = lax.rem(end + 3, n)
+        cot_all[1, i] = cot_own[end]
+
+        @pl.loop(0, width // TILE)
+        def _(k):
+            c = columns(k)
+            total = tn(mixed_all[first, :, c], cot_all[1, first])
+            total += tn(mixed_all[second, :, c], cot_all[1, second])
+            total += tn(mixed_all[third, :, c], cot_all[1, third])
+            end_out[c, :] = total.astype(jnp.bfloat16)
+
+        end_pass().start()
+
+    def w_used(side, s, inside, onward):
+        @pl.when(inside)
+        def _():
+            w_across_in(s).wait_recv()
+            use_weight(s)
+
+    use_weight(i)
 
     def round_of(k, carry):
         def w_arrives(side, s, inside, onward):
-            @pl.when(inside & (k < n))
+            @pl.when(inside)
             def _():
                 w_pass(side, s).wait_recv()
                 w_across(s).start()
@@ -311,47 +397,44 @@
                     w_pass(side, s).start()
 
         def m_arrives(side, s, inside, onward):
-            @pl.when(inside & (k >= 2))
+            @pl.when(inside & middle)
             def _():
                 m_pass(side, s).wait_recv()
 
-            @pl.when(onward)
-            def _():
-                m_pass(side, s).start()
-
-        def w_used(side, s, inside, onward):
-            first = inside if side == 0 else inside & (k >= 2)
-
-            @pl.when(first)
-            def _():
-                @pl.when(k >= 2)
+                @pl.when(m_onward(side, inside))
                 def _():
-                    w_across_in(s).wait_recv()
-
-                use_weight(s)
+                    m_pass(side, s).start()
 
         at_distance(k, w_arrives)
-
-        @pl.when(k < n)
+        at_distance(k, m_arrives)
+
+        @pl.when(k == 1)
         def _():
-            at_distance(k - 1, m_arrives)
-
-        at_distance(k - 1, w_used)
+            blocks_taken(share_cot)
+
+        @pl.when((k == n - 2) & beside_end)
+        def _():
+            end_terms()
+
+        at_distance(k, w_used)
         return carry
 
-    lax.fori_loop(1, n + 1, round_of, 0)
+    lax.fori_loop(1, n, round_of, 0)
 
     others(i, lambda j: rows_to(j).wait_send())
 
     @pl.loop(0, width // TILE)
     def _(k):
         c = columns(k)
-        chosen = choose_ref[:, c].astype(jnp.float32) > 0.5
+        chosen = choose_v[:, c].astype(jnp.float32) > 0.5
         grad = grad_acc[:, c]
         zero = jnp.zeros_like(grad)
         grad_base_ref[:, c] = jnp.where(chosen, zero, grad).astype(jnp.bfloat16)
-        swapped = jnp.where(chosen, grad, zero).astype(jnp.bfloat16)
-        rows_out[:, c] = nn(pick_back_ref[...], swapped).astype(jnp.bfloat16)
+        swapped_v[:, c] = jnp.where(chosen, grad, zero).astype(jnp.bfloat16)
+
+    @pl.loop(0, rows_out.shape[0] // TILE)
+    def _(k):
+        rows_out[columns(k), :] = tn(place_v[:, columns(k)], swapped_v[...]).astype(jnp.bfloat16)
 
     others(i, lambda j: rows_home(j).start())
     home_ref[slot_rows(i), :] = rows_out[slot_rows(i), :]
@@ -360,21 +443,9 @@
     def _(k):
         grad_weight_ref[columns(k), :] = tn(mixed_all[i, :, columns(k)], cot_own[i])
 
-    def tokens_of(k, carry):
-        def m_used(side, s, inside, onward):
-            @pl.when(inside)
-            def _():
-                @pl.when(k == n - 1)
-                def _():
-                    m_pass(side, s).wait_recv()
-
-                others(t, lambda u: cot_in(s, u).wait_recv())
-                use_tokens(s)
-
-        at_distance(k, m_used)
-        return carry
-
-    lax.fori_loop(1, n, tokens_of, 0)
+    @pl.when(middle)
+    def _():
+        others(i, use_tokens)
 
     others(t, lambda u: part_from(u).wait_recv())
     part_in[t] = part_out[t]
@@ -393,17 +464,33 @@
     @pl.loop(0, width // TILE)
     def _(k):
         c = columns(k)
-        grad_source_ref[:, c] = nn(place_back_ref[...], home_ref[:, c]).astype(jnp.bfloat16)
-
+        grad_source_ref[:, c] = nn(back_v[...], home_ref[:, c]).astype(jnp.bfloat16)
+
+    @pl.when(jnp.logical_not(middle))
+    def _():
+        end_pass().wait_recv()
+
+        @pl.loop(0, width // TILE)
+        def _(k):
+            grad_weight_ref[columns(k), :] += end_in[columns(k), :].astype(jnp.float32)
+
+    @pl.when(beside_end)
+    def _():
+        end_pass().wait_send()
+
+    cot_sent(lambda copy: copy.wait_send())
     others(i, lambda j: rows_home(j).wait_send())
     others(t, lambda u: part_to(u).wait_send())
-    others(i, lambda j: others(t, lambda u: cot_share(j, u).wait_send()))
+    blocks_taken(lambda kind, j: others(t, lambda u: cot_share(kind, j, u).wait_send()))
 
     def drain(k, carry):
         def sent(side, s, inside, onward):
             @pl.when(onward)
             def _():
                 w_pass(side, s).wait_send()
+
+            @pl.when(m_onward(side, inside) & (middle | (k == 0)))
+            def _():
                 m_pass(side, s).wait_send()
 
             @pl.when(inside & (k >= 1))
@@ -414,6 +501,15 @@
         return carry
 
     lax.fori_loop(0, n, drain, 0)
+
+
+def copy_out(*refs):
+    sem = refs[8]
+    copies = [pltpu.make_async_copy(refs[k], refs[4 + k], sem.at[k]) for k in range(4)]
+    for copy in copies:
+        copy.start()
+    for copy in copies:
+        copy.wait()
 
 
 def with_kernel(
@@ -424,23 +520,12 @@
     slots = n * send_slots.shape[2]
     depth, block = weight.shape
     prompts, heads_here = head_mask.shape
-    send_index = send_slots.reshape(-1)
-    recv_index = recv_slots.reshape(-1)
-    row = jnp.arange(rows, dtype=jnp.int32)
-    pick = (send_index[:, None] == row[None, :]).astype(jnp.bfloat16)
-    place_back = (row[:, None] == send_index[None, :]).astype(jnp.bfloat16)
-    place = (row[:, None] == recv_index[None, :]).astype(jnp.bfloat16)
-    pick_back = (recv_index[:, None] == row[None, :]).astype(jnp.bfloat16)
-    paired = jnp.any(row[:, None] == recv_index[None, :], axis=1)
-    swap = (paired.reshape(prompts, rows // prompts)[:, :, None] & (head_mask == 1)[:, None, :]).reshape(
-        rows, heads_here
-    )
-    choose = jnp.repeat(swap, width // heads_here, axis=1).astype(jnp.bfloat16)
+    heads = jnp.repeat(head_mask, width // heads_here, axis=1).astype(jnp.float32)
     kept = pl.BlockSpec(memory_space=pl.ANY)
     near = pl.BlockSpec(memory_space=pltpu.VMEM)
     dma = pltpu.SemaphoreType.DMA
     bf16 = jnp.bfloat16
-    return pl.pallas_call(
+    results = pl.pallas_call(
         functools.partial(fused, n),
         out_shape=(
             jax.ShapeDtypeStruct((rows, width), bf16),
@@ -448,12 +533,12 @@
             jax.ShapeDtypeStruct((rows, width), bf16),
             jax.ShapeDtypeStruct((depth, block), jnp.float32),
         ),
-        in_specs=[kept] * 3 + [near] * 7,
+        in_specs=[kept] * 3 + [near] * 5,
         out_specs=(near,) * 4,
         scratch_shapes=[
             pltpu.VMEM((n, depth, block), bf16),
             pltpu.VMEM((n, rows, block), bf16),
-            pltpu.VMEM((n, rows, block), bf16),
+            pltpu.VMEM((2, n, rows, block), bf16),
             pltpu.VMEM((n, rows, width), bf16),
             pltpu.VMEM((slots, width), bf16),
             pltpu.VMEM((slots, width), bf16),
@@ -462,6 +547,12 @@
             pltpu.VMEM((n, rows, block), bf16),
             pltpu.VMEM((rows, width), jnp.float32),
             pltpu.VMEM((rows, width), bf16),
+            pltpu.VMEM((rows, width), bf16),
+            pltpu.VMEM((rows, slots), bf16),
+            pltpu.VMEM((rows, slots), bf16),
+            pltpu.VMEM((rows, width), bf16),
+            pltpu.VMEM((depth, block), bf16),
+            pltpu.VMEM((depth, block), bf16),
             dma((n + 2,)),
             dma((2, n)),
             dma((n,)),
@@ -474,21 +565,38 @@
             dma((n,)),
             dma((n,)),
             dma((n,)),
-            dma((n, n)),
-            dma((n, n)),
-            dma((n,)),
-            dma((n,)),
+            dma((2, n, n)),
+            dma((2, n, n)),
+            dma((n,)),
+            dma((n,)),
+            dma((1,)),
+            dma((1,)),
         ],
         compiler_params=pltpu.CompilerParams(
             collective_id=0, has_side_effects=True, vmem_limit_bytes=60 * 1024 * 1024
         ),
     )(
-        weight, cotangent, residual, base_heads, source_heads, choose, pick, place, pick_back, place_back
+        weight,
+        cotangent,
+        residual,
+        base_heads,
+        source_heads,
+        send_slots.reshape(1, slots),
+        recv_slots.reshape(1, slots),
+        heads,
     )
+    return pl.pallas_call(
+        copy_out,
+        out_shape=tuple(jax.ShapeDtypeStruct(x.shape, x.dtype) for x in results),
+        in_specs=[kept] * 4,
+        out_specs=(kept,) * 4,
+        scratch_shapes=[dma((4,))],
+        compiler_params=pltpu.CompilerParams(vmem_limit_bytes=60 * 1024 * 1024),
+    )(*results)
 
 
 def solution(mesh):
-    square = mesh.shape["dp"] == mesh.shape["tensor"] and mesh.shape["group"] == 2
+    square = mesh.shape["dp"] == mesh.shape["tensor"] == 4 and mesh.shape["group"] == 2
     return jax.shard_map(
         with_kernel if square else with_collectives,
         mesh=mesh,

time: 241 us -> 451 us (1.87)
  Pallas kernels: 226 us -> 447 us
  local copies, waits for them, and re-layouts: 10.8 us -> 0.69 us
    pallas_call x0 -> x1, Pallas kernels: none -> 223 us  [with_kernel(): pl.pallas_call(copy_out, out_shape=tuple((jax.ShapeDtypeStruct(x.shape, x...]
    unnamed x7 -> x2, local copies, waits for them, and re-layouts: 10.2 us -> 0.69 us
where the time goes in v2:
time: 451 us; the launch traced here: 449 us
  Pallas kernels  447 us (99%)
    pallas_call x1, Pallas kernels, with_kernel(): pl.pallas_call(functools.partial(fused, n), out_shape=(jax.ShapeDtypeStru...  224 us
    pallas_call x1, Pallas kernels, with_kernel(): pl.pallas_call(copy_out, out_shape=tuple((jax.ShapeDtypeStruct(x.shape, x...  223 us

profile of v2, /device:TPU:3, one launch (start us, length us, event | category | flops | bytes accessed | tf_op | source)
XLA Modules:
  0.0 449.4 jit_solution(11020754894707079635)
XLA Ops:
  0.6 0.7 convert_element_type.5
  1.3 0.1 broadcast_bitcast_fusion
  1.4 0.6 copy.14
  2.0 223.9 %shard_map.111 = (bf16[512,1024]{1,0:T(8,128)(2,1)}, bf16[512,1024]{1,0:T(8,128)(2,1)}, bf16[512,1024]{1,0:T(8,128)(2,1)}, f32[1024,1024]{1,0:T(8,128)}) custom-call(bf16[1024,1024]{1,0:T(8,128)(2,1)} %weight_ref.1, bf16[512,4096]{1,0:T(8,128)(2,1)} %cotangent_ref.1, bf16[512,1024]{1,0:T(8,128)(2,1)} %residual_ref.1, bf16[512,1024]{1,0:T(8,128)(2,1)} %base_ref.1, ...), custom_call_target="tpu_custom_call" | custom-call | tf_op jit(solution)/shard_map/pallas_call | solution.py:528
  225.9 223.5 %shard_map.112 = (bf16[512,1024]{1,0:T(8,128)(2,1)}, bf16[512,1024]{1,0:T(8,128)(2,1)}, bf16[512,1024]{1,0:T(8,128)(2,1)}, f32[1024,1024]{1,0:T(8,128)}) custom-call(bf16[512,1024]{1,0:T(8,128)(2,1)} %get-tuple-element.8.refs_0_, bf16[512,1024]{1,0:T(8,128)(2,1)} %get-tuple-element.9.refs_1_, bf16[512,1024]{1,0:T(8,128)(2,1)} %get-tuple-element.10.refs_2_, ...), custom_call_target="tpu_custom_call" | custom-call | tf_op jit(solution)/shard_map/pallas_call | solution.py:588

commit v3 on v2

--- a/solution.py
+++ b/solution.py
@@ -214,8 +214,8 @@
             {"dp": taker},
         )
 
-    def cot_sent(body):
-        for b in range(n):
+    def cot_sent(body, blocks):
+        for b in blocks:
             taker = min(max(b, 1), n - 2)
 
             @pl.when((i != b) & (i != taker))
@@ -290,7 +290,6 @@
             w_first(side).start()
 
     at_distance(0, start_w)
-    cot_sent(lambda copy: copy.start())
     rows_in[slot_rows(i), :] = rows_out[slot_rows(i), :]
     place = hot(recv_ref[...])
     place_v[...] = place.astype(jnp.bfloat16)
@@ -319,25 +318,22 @@
         def _():
             m_pass(side, s).start()
 
-    at_distance(0, start_m)
     for load in loads:
         load.wait()
 
-    def blocks_taken(body):
-        for kind in range(2):
-
-            @pl.when(middle if kind == 0 else beside_end)
-            def _():
-                def one(j):
-                    if kind == 0:
+    def blocks_taken(kind, body):
+        @pl.when(middle if kind == 0 else beside_end)
+        def _():
+            def one(j):
+                if kind == 0:
+                    body(kind, j)
+                else:
+
+                    @pl.when(j != end)
+                    def _():
                         body(kind, j)
-                    else:
-
-                        @pl.when(j != end)
-                        def _():
-                            body(kind, j)
-
-                others(i, one)
+
+            others(i, one)
 
     def share_cot(kind, j):
         cot_in(kind, j, t).wait_recv()
@@ -355,13 +351,15 @@
             part_to(s).start()
 
     def use_tokens(j):
+        others(t, lambda u: cot_in(0, j, u).wait_recv())
+
         @pl.loop(0, width // TILE)
         def _(k):
             c = columns(k)
             grad_weight_ref[c, :] += tn(mixed_all[j, :, c], cot_all[0, j])
 
     def end_terms():
-        blocks_taken(lambda kind, j: others(t, lambda u: cot_in(kind, j, u).wait_recv()))
+        blocks_taken(1, lambda kind, j: others(t, lambda u: cot_in(kind, j, u).wait_recv()))
         first = lax.rem(end + 1, n)
         second = lax.rem(end + 2, n)
         third = lax.rem(end + 3, n)
@@ -383,43 +381,45 @@
             w_across_in(s).wait_recv()
             use_weight(s)
 
+    def w_arrives(side, s, inside, onward):
+        @pl.when(inside)
+        def _():
+            w_pass(side, s).wait_recv()
+
+            @pl.when(onward)
+            def _():
+                w_pass(side, s).start()
+
+            w_across(s).start()
+
+    def m_arrives(side, s, inside, onward):
+        @pl.when(inside & middle)
+        def _():
+            m_pass(side, s).wait_recv()
+
+            @pl.when(m_onward(side, inside))
+            def _():
+                m_pass(side, s).start()
+
+    at_distance(1, w_arrives)
+    at_distance(0, start_m)
+    cot_sent(lambda copy: copy.start(), (0, n - 1))
     use_weight(i)
-
-    def round_of(k, carry):
-        def w_arrives(side, s, inside, onward):
-            @pl.when(inside)
-            def _():
-                w_pass(side, s).wait_recv()
-                w_across(s).start()
-
-                @pl.when(onward)
-                def _():
-                    w_pass(side, s).start()
-
-        def m_arrives(side, s, inside, onward):
-            @pl.when(inside & middle)
-            def _():
-                m_pass(side, s).wait_recv()
-
-                @pl.when(m_onward(side, inside))
-                def _():
-                    m_pass(side, s).start()
-
-        at_distance(k, w_arrives)
-        at_distance(k, m_arrives)
-
-        @pl.when(k == 1)
-        def _():
-            blocks_taken(share_cot)
-
-        @pl.when((k == n - 2) & beside_end)
-        def _():
-            end_terms()
-
-        at_distance(k, w_used)
-        return carry
-
-    lax.fori_loop(1, n, round_of, 0)
+    at_distance(2, w_arrives)
+    at_distance(1, m_arrives)
+    cot_sent(lambda copy: copy.start(), range(1, n - 1))
+    at_distance(1, w_used)
+    blocks_taken(1, share_cot)
+    at_distance(3, w_arrives)
+    at_distance(2, w_used)
+    at_distance(2, m_arrives)
+
+    @pl.when(beside_end)
+    def _():
+        end_terms()
+
+    blocks_taken(0, share_cot)
+    at_distance(3, w_used)
 
     others(i, lambda j: rows_to(j).wait_send())
 
@@ -478,10 +478,11 @@
     def _():
         end_pass().wait_send()
 
-    cot_sent(lambda copy: copy.wait_send())
+    cot_sent(lambda copy: copy.wait_send(), range(n))
     others(i, lambda j: rows_home(j).wait_send())
     others(t, lambda u: part_to(u).wait_send())
-    blocks_taken(lambda kind, j: others(t, lambda u: cot_share(kind, j, u).wait_send()))
+    for kind in range(2):
+        blocks_taken(kind, lambda kind, j: others(t, lambda u: cot_share(kind, j, u).wait_send()))
 
     def drain(k, carry):
         def sent(side, s, inside, onward):
@@ -504,12 +505,8 @@
 
 
 def copy_out(*refs):
-    sem = refs[8]
-    copies = [pltpu.make_async_copy(refs[k], refs[4 + k], sem.at[k]) for k in range(4)]
-    for copy in copies:
-        copy.start()
-    for copy in copies:
-        copy.wait()
+    for k in range(4):
+        refs[4 + k][...] = refs[k][...]
 
 
 def with_kernel(
@@ -585,12 +582,14 @@
         recv_slots.reshape(1, slots),
         heads,
     )
+    steps = 4
+    blocks = [pl.BlockSpec((x.shape[0] // steps, x.shape[1]), lambda k: (k, 0)) for x in results]
     return pl.pallas_call(
         copy_out,
+        grid=(steps,),
         out_shape=tuple(jax.ShapeDtypeStruct(x.shape, x.dtype) for x in results),
-        in_specs=[kept] * 4,
-        out_specs=(kept,) * 4,
-        scratch_shapes=[dma((4,))],
+        in_specs=blocks,
+        out_specs=tuple(blocks),
         compiler_params=pltpu.CompilerParams(vmem_limit_bytes=60 * 1024 * 1024),
     )(*results)
 

time: 451 us -> 235 us (0.52)
  Pallas kernels: 447 us -> 233 us
    pallas_call x1, Pallas kernels: 223 us -> 6.46 us  [with_kernel(): pl.pallas_call(copy_out, grid=(steps,), out_shape=tuple((jax.ShapeDtypeSt...]
where the time goes in v3:
time: 235 us
  Pallas kernels  233 us (99%)
    pallas_call x1, Pallas kernels, with_kernel(): pl.pallas_call(functools.partial(fused, n), out_shape=(jax.ShapeDtypeStru...  227 us
    pallas_call x1, Pallas kernels, with_kernel(): pl.pallas_call(copy_out, grid=(steps,), out_shape=tuple((jax.ShapeDtypeSt...  6.46 us

profile of v3, /device:TPU:3, one launch (start us, length us, event | category | flops | bytes accessed | tf_op | source)
XLA Modules:
  0.0 235.0 jit_solution(3632901761861420149)
XLA Ops:
  0.6 0.7 convert_element_type.5
  1.3 0.1 broadcast_bitcast_fusion
  1.4 0.6 copy.14
  2.0 226.6 %shard_map.111 = (bf16[512,1024]{1,0:T(8,128)(2,1)}, bf16[512,1024]{1,0:T(8,128)(2,1)}, bf16[512,1024]{1,0:T(8,128)(2,1)}, f32[1024,1024]{1,0:T(8,128)}) custom-call(bf16[1024,1024]{1,0:T(8,128)(2,1)} %weight_ref.1, bf16[512,4096]{1,0:T(8,128)(2,1)} %cotangent_ref.1, bf16[512,1024]{1,0:T(8,128)(2,1)} %residual_ref.1, bf16[512,1024]{1,0:T(8,128)(2,1)} %base_ref.1, ...), custom_call_target="tpu_custom_call" | custom-call | tf_op jit(solution)/shard_map/pallas_call | solution.py:525
  228.6 6.5 %shard_map.112 = (bf16[512,1024]{1,0:T(8,128)(2,1)}, bf16[512,1024]{1,0:T(8,128)(2,1)}, bf16[512,1024]{1,0:T(8,128)(2,1)}, f32[1024,1024]{1,0:T(8,128)}) custom-call(bf16[512,1024]{1,0:T(8,128)(2,1)} %get-tuple-element.8.refs_0_, bf16[512,1024]{1,0:T(8,128)(2,1)} %get-tuple-element.9.refs_1_, bf16[512,1024]{1,0:T(8,128)(2,1)} %get-tuple-element.10.refs_2_, ...), custom_call_target="tpu_custom_call" | custom-call | tf_op jit(solution)/shard_map/pallas_call | solution.py:587

commit v4 on v3

--- a/solution.py
+++ b/solution.py
@@ -112,8 +112,6 @@
     place_v,
     back_v,
     swapped_v,
-    end_out,
-    end_in,
     local_sem,
     w_send,
     w_recv,
@@ -130,8 +128,6 @@
     b_send,
     p_send,
     p_recv,
-    e_send,
-    e_recv,
 ):
     g = lax.axis_index("group")
     i = lax.axis_index("dp")
@@ -141,9 +137,6 @@
     block = w_all.shape[2]
     slots = rows_out.shape[0] // n
     quarter = tokens // n
-    middle = (i >= 1) & (i <= n - 2)
-    beside_end = (i == 1) | (i == n - 2)
-    end = jnp.where(i <= 1, 0, n - 1)
 
     def remote(src, dst, send, recv, to):
         return pltpu.make_async_remote_copy(
@@ -204,8 +197,8 @@
         return remote(rows_out.at[slot_rows(j), :], home_ref.at[slot_rows(j), :], h_send.at[j], h_recv.at[j], {"dp": j})
 
     def cot_to(b):
-        kind = 0 if 0 < b < n - 1 else 1
-        taker = min(max(b, 1), n - 2)
+        kind = 0
+        taker = b
         return remote(
             cotangent_ref.at[strip(t), b * block : (b + 1) * block],
             cot_all.at[kind, i, strip(t), :],
@@ -216,9 +209,8 @@
 
     def cot_sent(body, blocks):
         for b in blocks:
-            taker = min(max(b, 1), n - 2)
-
-            @pl.when((i != b) & (i != taker))
+
+            @pl.when(i != b)
             def _():
                 body(cot_to(b))
 
@@ -229,9 +221,6 @@
     def cot_in(kind, j, u):
         piece = cot_all.at[kind, j, strip(u), :]
         return remote(piece, piece, b_send.at[kind, j, u], c_recv.at[kind, j, u], {"tensor": u})
-
-    def end_pass():
-        return remote(end_out, end_in, e_send.at[0], e_recv.at[0], {"dp": end})
 
     def part_to(u):
         return remote(part_out.at[u], part_in.at[t], p_send.at[u], p_recv.at[t], {"tensor": u})
@@ -311,7 +300,7 @@
         grad_acc[:, c] = jnp.zeros((tokens, TILE), jnp.float32)
 
     def m_onward(side, inside):
-        return inside & ((i + 1 <= n - 2) if side == 0 else (i - 1 >= 1))
+        return inside & ((i + 1 < n) if side == 0 else (i >= 1))
 
     def start_m(side, s, inside, onward):
         @pl.when(m_onward(side, inside))
@@ -322,18 +311,7 @@
         load.wait()
 
     def blocks_taken(kind, body):
-        @pl.when(middle if kind == 0 else beside_end)
-        def _():
-            def one(j):
-                if kind == 0:
-                    body(kind, j)
-                else:
-
-                    @pl.when(j != end)
-                    def _():
-                        body(kind, j)
-
-            others(i, one)
+        others(i, lambda j: body(kind, j))
 
     def share_cot(kind, j):
         cot_in(kind, j, t).wait_recv()
@@ -358,22 +336,10 @@
             c = columns(k)
             grad_weight_ref[c, :] += tn(mixed_all[j, :, c], cot_all[0, j])
 
-    def end_terms():
-        blocks_taken(1, lambda kind, j: others(t, lambda u: cot_in(kind, j, u).wait_recv()))
-        first = lax.rem(end + 1, n)
-        second = lax.rem(end + 2, n)
-        third = lax.rem(end + 3, n)
-        cot_all[1, i] = cot_own[end]
-
-        @pl.loop(0, width // TILE)
-        def _(k):
-            c = columns(k)
-            total = tn(mixed_all[first, :, c], cot_all[1, first])
-            total += tn(mixed_all[second, :, c], cot_all[1, second])
-            total += tn(mixed_all[third, :, c], cot_all[1, third])
-            end_out[c, :] = total.astype(jnp.bfloat16)
-
-        end_pass().start()
+    def m_used(side, s, inside, onward):
+        @pl.when(inside)
+        def _():
+            use_tokens(s)
 
     def w_used(side, s, inside, onward):
         @pl.when(inside)
@@ -393,7 +359,7 @@
             w_across(s).start()
 
     def m_arrives(side, s, inside, onward):
-        @pl.when(inside & middle)
+        @pl.when(inside)
         def _():
             m_pass(side, s).wait_recv()
 
@@ -409,14 +375,9 @@
     at_distance(1, m_arrives)
     cot_sent(lambda copy: copy.start(), range(1, n - 1))
     at_distance(1, w_used)
-    blocks_taken(1, share_cot)
     at_distance(3, w_arrives)
     at_distance(2, w_used)
     at_distance(2, m_arrives)
-
-    @pl.when(beside_end)
-    def _():
-        end_terms()
 
     blocks_taken(0, share_cot)
     at_distance(3, w_used)
@@ -443,9 +404,10 @@
     def _(k):
         grad_weight_ref[columns(k), :] = tn(mixed_all[i, :, columns(k)], cot_own[i])
 
-    @pl.when(middle)
-    def _():
-        others(i, use_tokens)
+    at_distance(1, m_used)
+    at_distance(2, m_used)
+    at_distance(3, m_arrives)
+    at_distance(3, m_used)
 
     others(t, lambda u: part_from(u).wait_recv())
     part_in[t] = part_out[t]
@@ -466,22 +428,10 @@
         c = columns(k)
         grad_source_ref[:, c] = nn(back_v[...], home_ref[:, c]).astype(jnp.bfloat16)
 
-    @pl.when(jnp.logical_not(middle))
-    def _():
-        end_pass().wait_recv()
-
-        @pl.loop(0, width // TILE)
-        def _(k):
-            grad_weight_ref[columns(k), :] += end_in[columns(k), :].astype(jnp.float32)
-
-    @pl.when(beside_end)
-    def _():
-        end_pass().wait_send()
-
     cot_sent(lambda copy: copy.wait_send(), range(n))
     others(i, lambda j: rows_home(j).wait_send())
     others(t, lambda u: part_to(u).wait_send())
-    for kind in range(2):
+    for kind in range(1):
         blocks_taken(kind, lambda kind, j: others(t, lambda u: cot_share(kind, j, u).wait_send()))
 
     def drain(k, carry):
@@ -490,7 +440,7 @@
             def _():
                 w_pass(side, s).wait_send()
 
-            @pl.when(m_onward(side, inside) & (middle | (k == 0)))
+            @pl.when(m_onward(side, inside) & (k < n))
             def _():
                 m_pass(side, s).wait_send()
 
@@ -535,7 +485,7 @@
         scratch_shapes=[
             pltpu.VMEM((n, depth, block), bf16),
             pltpu.VMEM((n, rows, block), bf16),
-            pltpu.VMEM((2, n, rows, block), bf16),
+            pltpu.VMEM((1, n, rows, block), bf16),
             pltpu.VMEM((n, rows, width), bf16),
             pltpu.VMEM((slots, width), bf16),
             pltpu.VMEM((slots, width), bf16),
@@ -548,8 +498,6 @@
             pltpu.VMEM((rows, slots), bf16),
             pltpu.VMEM((rows, slots), bf16),
             pltpu.VMEM((rows, width), bf16),
-            pltpu.VMEM((depth, block), bf16),
-            pltpu.VMEM((depth, block), bf16),
             dma((n + 2,)),
             dma((2, n)),
             dma((n,)),
@@ -562,12 +510,10 @@
             dma((n,)),
             dma((n,)),
             dma((n,)),
-            dma((2, n, n)),
-            dma((2, n, n)),
-            dma((n,)),
-            dma((n,)),
-            dma((1,)),
-            dma((1,)),
+            dma((1, n, n)),
+            dma((1, n, n)),
+            dma((n,)),
+            dma((n,)),
         ],
         compiler_params=pltpu.CompilerParams(
             collective_id=0, has_side_effects=True, vmem_limit_bytes=60 * 1024 * 1024

time: 235 us -> 236 us (level)
  no operation moved by 1% of the time
where the time goes in v4:
time: 236 us
  Pallas kernels  234 us (99%)
    pallas_call x1, Pallas kernels, with_kernel(): pl.pallas_call(functools.partial(fused, n), out_shape=(jax.ShapeDtypeStru...  228 us
    pallas_call x1, Pallas kernels, with_kernel(): pl.pallas_call(copy_out, grid=(steps,), out_shape=tuple((jax.ShapeDtypeSt...  6.46 us

profile of v4, /device:TPU:3, one launch (start us, length us, event | category | flops | bytes accessed | tf_op | source)
XLA Modules:
  0.0 236.0 jit_solution(1431194924964475429)
XLA Ops:
  0.6 0.7 convert_element_type.5
  1.3 0.1 broadcast_bitcast_fusion
  1.4 0.6 copy.14
  2.0 227.6 %shard_map.111 = (bf16[512,1024]{1,0:T(8,128)(2,1)}, bf16[512,1024]{1,0:T(8,128)(2,1)}, bf16[512,1024]{1,0:T(8,128)(2,1)}, f32[1024,1024]{1,0:T(8,128)}) custom-call(bf16[1024,1024]{1,0:T(8,128)(2,1)} %weight_ref.1, bf16[512,4096]{1,0:T(8,128)(2,1)} %cotangent_ref.1, bf16[512,1024]{1,0:T(8,128)(2,1)} %residual_ref.1, bf16[512,1024]{1,0:T(8,128)(2,1)} %base_ref.1, ...), custom_call_target="tpu_custom_call" | custom-call | tf_op jit(solution)/shard_map/pallas_call | solution.py:475
  229.6 6.5 %shard_map.112 = (bf16[512,1024]{1,0:T(8,128)(2,1)}, bf16[512,1024]{1,0:T(8,128)(2,1)}, bf16[512,1024]{1,0:T(8,128)(2,1)}, f32[1024,1024]{1,0:T(8,128)}) custom-call(bf16[512,1024]{1,0:T(8,128)(2,1)} %get-tuple-element.8.refs_0_, bf16[512,1024]{1,0:T(8,128)(2,1)} %get-tuple-element.9.refs_1_, bf16[512,1024]{1,0:T(8,128)(2,1)} %get-tuple-element.10.refs_2_, ...), custom_call_target="tpu_custom_call" | custom-call | tf_op jit(solution)/shard_map/pallas_call | solution.py:533

commit v5 on v3

--- a/solution.py
+++ b/solution.py
@@ -405,6 +405,11 @@
     at_distance(0, start_m)
     cot_sent(lambda copy: copy.start(), (0, n - 1))
     use_weight(i)
+
+    @pl.loop(0, width // TILE)
+    def _(k):
+        grad_weight_ref[columns(k), :] = tn(mixed_all[i, :, columns(k)], cot_own[i])
+
     at_distance(2, w_arrives)
     at_distance(1, m_arrives)
     cot_sent(lambda copy: copy.start(), range(1, n - 1))
@@ -412,13 +417,13 @@
     blocks_taken(1, share_cot)
     at_distance(3, w_arrives)
     at_distance(2, w_used)
+    blocks_taken(0, share_cot)
     at_distance(2, m_arrives)
 
     @pl.when(beside_end)
     def _():
         end_terms()
 
-    blocks_taken(0, share_cot)
     at_distance(3, w_used)
 
     others(i, lambda j: rows_to(j).wait_send())
@@ -438,10 +443,6 @@
 
     others(i, lambda j: rows_home(j).start())
     home_ref[slot_rows(i), :] = rows_out[slot_rows(i), :]
-
-    @pl.loop(0, width // TILE)
-    def _(k):
-        grad_weight_ref[columns(k), :] = tn(mixed_all[i, :, columns(k)], cot_own[i])
 
     @pl.when(middle)
     def _():
@@ -582,7 +583,7 @@
         recv_slots.reshape(1, slots),
         heads,
     )
-    steps = 4
+    steps = 8
     blocks = [pl.BlockSpec((x.shape[0] // steps, x.shape[1]), lambda k: (k, 0)) for x in results]
     return pl.pallas_call(
         copy_out,

time: 235 us -> 237 us (level)
  no operation moved by 1% of the time
where the time goes in v5:
time: 237 us
  Pallas kernels  235 us (99%)
    pallas_call x1, Pallas kernels, with_kernel(): pl.pallas_call(functools.partial(fused, n), out_shape=(jax.ShapeDtypeStru...  227 us
    pallas_call x1, Pallas kernels, with_kernel(): pl.pallas_call(copy_out, grid=(steps,), out_shape=tuple((jax.ShapeDtypeSt...  8.36 us

profile of v5, /device:TPU:3, one launch (start us, length us, event | category | flops | bytes accessed | tf_op | source)
XLA Modules:
  0.0 236.9 jit_solution(12825201235981883838)
XLA Ops:
  0.6 0.7 convert_element_type.5
  1.3 0.1 broadcast_bitcast_fusion
  1.4 0.6 copy.14
  2.0 226.5 %shard_map.111 = (bf16[512,1024]{1,0:T(8,128)(2,1)}, bf16[512,1024]{1,0:T(8,128)(2,1)}, bf16[512,1024]{1,0:T(8,128)(2,1)}, f32[1024,1024]{1,0:T(8,128)}) custom-call(bf16[1024,1024]{1,0:T(8,128)(2,1)} %weight_ref.1, bf16[512,4096]{1,0:T(8,128)(2,1)} %cotangent_ref.1, bf16[512,1024]{1,0:T(8,128)(2,1)} %residual_ref.1, bf16[512,1024]{1,0:T(8,128)(2,1)} %base_ref.1, ...), custom_call_target="tpu_custom_call" | custom-call | tf_op jit(solution)/shard_map/pallas_call | solution.py:526
  228.5 8.4 %shard_map.112 = (bf16[512,1024]{1,0:T(8,128)(2,1)}, bf16[512,1024]{1,0:T(8,128)(2,1)}, bf16[512,1024]{1,0:T(8,128)(2,1)}, f32[1024,1024]{1,0:T(8,128)}) custom-call(bf16[512,1024]{1,0:T(8,128)(2,1)} %get-tuple-element.8.refs_0_, bf16[512,1024]{1,0:T(8,128)(2,1)} %get-tuple-element.9.refs_1_, bf16[512,1024]{1,0:T(8,128)(2,1)} %get-tuple-element.10.refs_2_, ...), custom_call_target="tpu_custom_call" | custom-call | tf_op jit(solution)/shard_map/pallas_call | solution.py:588
